TPU v7x, 512 devices: a whole 4x8x8 slice. The times are simulated.
512 devices in a mesh: leaf: 128 (over z, y, core), lvl: 4 (over x).
Axes of the slice: x: 4, y: 8, z: 8, core: 2. Of those that a mesh axis runs over, the one named last changes fastest.
Arguments:
- charges: bfloat16 [8192, 512], P('leaf', 'lvl'), may hold values from -6 to 6
- p2m_matrix: bfloat16 [512, 512], P('lvl'), may hold values from -0.25 to 0.25
- m2m_matrices: bfloat16 [8, 512, 512], P(None, None, 'lvl'), may hold values from -0.09375 to 0.09375
- leaf_ops: bfloat16 [8, 512, 512], P(None, None, 'lvl'), may hold values from -0.0546875 to 0.0546875
- coarse_ops: bfloat16 [4, 512, 512], P(None, None, 'lvl'), may hold values from -0.0546875 to 0.0546875
- l2l_matrices: bfloat16 [8, 512, 512], P(None, None, 'lvl'), may hold values from -0.25 to 0.25
- l2p_matrix: bfloat16 [512, 512], replicated, may hold values from -0.25 to 0.25
- near_kernel_tiles: bfloat16 [4, 512, 512], P(None, None, 'lvl'), may hold values from -0.09375 to 0.09375
- send_rows: int32 [128, 128, 4], P('leaf'), may hold values from 0 to 63
- m2l_src: int32 [8192, 24], P('leaf'), may hold values from 0 to 575, as said below
- m2l_op: int32 [8192, 24], P('leaf'), may hold values from 0 to 7
- m2l_count: int32 [8192], P('leaf'), may hold values from 12 to 24
- coarse_src: int32 [1024, 24], P('leaf'), may hold values from 0 to 1023
- coarse_op: int32 [1024, 24], P('leaf'), may hold values from 0 to 3
- near_src: int32 [8192, 8], P('leaf'), may hold values from 0 to 8191, as said below
- neighbour_kernel_type: int32 [8192, 8], P('leaf'), may hold values from 0 to 3
Outputs:
- potential: float32 [8192, 512], P('leaf', 'lvl')
Inputs may be any that keep to these rules, and one draw needn't show every extreme that they name: `send_rows`: a local leaf index of the sending device. `m2l_src`: an index into pool_d of the leaf's block; on each block every one of the 576 entries is named in some slot below 12. `near_src`: a neighbour lies within 32 leaves of its target in Morton order.
All inputs are finite; a program needn't handle non-finite values.
Results may differ from a plain program's by a relative error of at most 0.018.
Values may be sent and summed in bfloat16 or wider, within the bound.
A program may use at most 64 MiB of HBM per device.

v0:
```python
import jax
import jax.numpy as jnp
from jax import lax
from jax.sharding import PartitionSpec as P


def with_halo(value, sides, width):
    for axis, dim in sides:
        size, length = (lax.axis_size(axis), value.shape[dim])
        up = [(i, (i + 1) % size) for i in range(size - 1)]
        down = [(j, i) for i, j in up]
        last = lax.slice_in_dim(value, length - width, length, axis=dim)
        initial = lax.slice_in_dim(value, 0, width, axis=dim)
        before = lax.ppermute(last, axis, up)
        after = lax.ppermute(initial, axis, down)
        value = jnp.concatenate([before, value, after], axis=dim)
    return value


def local(
    charges,
    p2m_matrix,
    m2m_matrices,
    leaf_ops,
    coarse_ops,
    l2l_matrices,
    l2p_matrix,
    near_kernel_tiles,
    send_rows,
    m2l_src,
    m2l_op,
    m2l_count,
    coarse_src,
    coarse_op,
    near_src,
    neighbour_kernel_type,
):
    leaf_count = charges.shape[0]
    width = p2m_matrix.shape[1]
    quarter = leaf_ops.shape[2]
    point_part = near_kernel_tiles.shape[2]
    level_index = lax.axis_index("lvl")
    block_index = lax.axis_index("leaf")
    all_points = lax.all_gather(charges, "lvl", axis=1, tiled=True)
    partial_value = jnp.dot(charges, p2m_matrix, preferred_element_type=jnp.float32)
    moments = lax.psum(partial_value.astype(jnp.bfloat16), "lvl")
    children = moments.reshape(leaf_count // 8, 8, width)
    parent_part = jnp.einsum(
        "cok,okj->cj", children, m2m_matrices, preferred_element_type=jnp.float32
    ).astype(jnp.bfloat16)
    parents = lax.all_gather(parent_part, "lvl", axis=1, tiled=True)
    coarse_all = lax.all_gather(parents, "leaf", axis=0, tiled=True)
    coarse_rows = coarse_all[coarse_src.reshape(-1)]
    coarse_ids = coarse_op.reshape(-1)
    selector = coarse_ids[None, :] == jnp.arange(coarse_ops.shape[0], dtype=jnp.int32)[:, None]
    spread = jnp.where(selector[:, :, None], coarse_rows[None], jnp.zeros((), jnp.bfloat16))
    coarse_terms = jnp.einsum("tek,tkj->ej", spread, coarse_ops, preferred_element_type=jnp.float32)
    coarse_part = jnp.sum(
        coarse_terms.reshape(coarse_src.shape[0], coarse_src.shape[1], quarter), axis=1
    ).astype(jnp.bfloat16)
    parent_local = lax.all_gather(coarse_part, "lvl", axis=1, tiled=True)
    down_part = jnp.einsum(
        "ck,okj->coj", parent_local, l2l_matrices, preferred_element_type=jnp.float32
    ).reshape(leaf_count, quarter)
    outgoing = moments[send_rows[0].reshape(-1)]
    received = lax.all_to_all(outgoing, "leaf", split_axis=0, concat_axis=0, tiled=True)
    pool = jnp.concatenate([moments, received], 0)
    pool_size = pool.shape[0]
    table = jnp.einsum("pk,tkj->tpj", pool, leaf_ops, preferred_element_type=jnp.float32)
    flat_table = table.reshape(leaf_ops.shape[0] * pool_size, quarter)
    flat_index = m2l_op * pool_size + m2l_src
    picked = flat_table[flat_index]
    live = jnp.arange(m2l_src.shape[1], dtype=jnp.int32)[None, :] < m2l_count[:, None]
    leaf_far = jnp.sum(jnp.where(live[:, :, None], picked, 0.0), axis=1)
    local_part = (leaf_far + down_part).astype(jnp.bfloat16)
    local_full = lax.all_gather(local_part, "lvl", axis=1, tiled=True)
    l2p_cols = lax.dynamic_slice_in_dim(l2p_matrix, level_index * point_part, point_part, 1)
    far = jnp.dot(local_full, l2p_cols, preferred_element_type=jnp.float32)
    reach = leaf_count // 2
    extended = with_halo(all_points, (("leaf", 0),), reach)
    span = extended.shape[0]
    tile_table = jnp.einsum(
        "rp,tpq->trq", extended, near_kernel_tiles, preferred_element_type=jnp.float32
    )
    first_leaf = block_index * leaf_count - reach
    near_index = neighbour_kernel_type * span + (near_src - first_leaf)
    near_rows = tile_table.reshape(near_kernel_tiles.shape[0] * span, point_part)[near_index]
    near = jnp.sum(near_rows, axis=1)
    return far + near


def solution(mesh):
    placed = (
        P("leaf", "lvl"),
        P("lvl", None),
        P(None, None, "lvl"),
        P(None, None, "lvl"),
        P(None, None, "lvl"),
        P(None, None, "lvl"),
        P(),
        P(None, None, "lvl"),
        P("leaf", None, None),
        P("leaf", None),
        P("leaf", None),
        P("leaf"),
        P("leaf", None),
        P("leaf", None),
        P("leaf", None),
        P("leaf", None),
    )
    return jax.shard_map(
        local, mesh=mesh, in_specs=placed, out_specs=P("leaf", "lvl"), check_vma=False
    )
```

profile of v0, /device:TPU:1, one launch (start us, length us, event | category | flops | bytes accessed | tf_op | source)
XLA Modules:
  0.0 193.6 jit_solution(11932699665940220869)
XLA Ops:
  6.5 0.0 copy-start
  6.5 0.0 all-reduce.2.cloned.1.call-start
  6.5 1.8 convolution_convert_fusion
  8.3 0.0 all-reduce.2.cloned.1.call-update
  8.4 0.0 all-gather.2.cloned.1.call-start
  8.4 9.5 %all_gather.19 = bf16[64,512]{1,0:T(8,128)(2,1)S(1)} all-gather(bf16[64,128]{1,0:T(8,128)(2,1)} %param.16), channel_id=1, replica_groups=mesh['leaf'=128,'lvl'=4] {'lvl'}, dimensions={1}, use_global_device_ids=true | all-gather | bytes 81920 | tf_op jit(solution)/shard_map/all_gather | solution.py:44
  18.0 6.4 %collective-permute-start = (bf16[32,512]{1,0:T(8,128)(2,1)S(1)}, bf16[32,512]{1,0:T(8,128)(2,1)S(1)}, u32[]{:S(2)}, u32[]{:S(2)}) collective-permute-start(bf16[32,512]{1,0:T(8,128)(2,1)S(1)} %get-tuple-element.5), channel_id=1, source_target_pairs={{0,4},{4,8},{8,12},{12,16},{16,20},{20,24},{24,28},{28,32},{32,36}... | collective-permute-start | bytes 98312 | tf_op jit(solution)/shard_map/ppermute | solution.py:14
  24.4 4.8 %collective-permute-start.1 = (bf16[32,512]{1,0:T(8,128)(2,1)S(1)}, bf16[32,512]{1,0:T(8,128)(2,1)S(1)}, u32[]{:S(2)}, u32[]{:S(2)}) collective-permute-start(bf16[32,512]{1,0:T(8,128)(2,1)S(1)} %get-tuple-element.6), channel_id=1, source_target_pairs={{4,0},{8,4},{12,8},{16,12},{20,16},{24,20},{28,24},{32,28},{36,32}... | collective-permute-start | bytes 98312 | tf_op jit(solution)/shard_map/ppermute | solution.py:15
  29.2 0.8 copy.17
  30.0 0.1 reshape_squeeze.3
  30.1 0.8 reshape.121
  30.9 33.8 %all-reduce.2.cloned.1.call-done = bf16[64,512]{1,0:T(8,128)(2,1)} async-done(((bf16[64,512]{1,0:T(8,128)(2,1)}), bf16[64,512]{1,0:T(8,128)(2,1)}) %all-reduce.2.cloned.1.call-update) | async-done | bytes 65552 | tf_op jit(solution)/shard_map/psum | solution.py:46
  64.7 1.5 fusion
  66.2 8.4 %all_gather.15 = bf16[8,512]{1,0:T(8,128)(2,1)} all-gather(bf16[8,128]{1,0:T(8,128)(2,1)S(1)} %fusion), channel_id=1, replica_groups=mesh['leaf'=128,'lvl'=4] {'lvl'}, dimensions={1}, use_global_device_ids=true | all-gather | bytes 10240 | tf_op jit(solution)/shard_map/all_gather | solution.py:51
  74.6 0.0 all-gather.2.cloned.1.call-update
  74.7 0.7 compare_select_fusion.2
  75.4 0.7 compare_select_fusion
  76.1 0.0 copy-done.1
  76.1 0.0 copy-start.4
  76.1 0.0 copy-start.5
  76.2 0.0 copy-start.3
  76.2 2.0 %gather_fusion = bf16[512,512]{1,0:T(8,128)(2,1)S(1)} fusion(bf16[64,512]{1,0:T(8,128)(2,1)S(1)} %copy-done.1, s32[1024]{0:T(1024)S(1)} %pad_clamp_fusion.3), kind=kCustom, calls=%fused_computation | custom fusion | bytes 1050624 | tf_op jit(solution)/shard_map/gather | solution.py:65
  78.2 0.9 all_to_all.8
  79.1 18.6 %all-to-all-start = ((bf16[128,4,512]{2,1,0:T(4,128)(2,1)}), bf16[128,4,512]{2,1,0:T(4,128)(2,1)S(1)}, u32[]{:S(2)}, u32[]{:S(2)}) async-start(bf16[128,4,512]{2,1,0:T(4,128)(2,1)} %all_to_all.8), calls=%async_computation | async-start | bytes 1048576 | tf_op jit(solution)/shard_map/all_to_all | solution.py:66
  97.7 0.1 copy.18
  97.8 0.1 reshape.135
  97.9 0.1 eq.19
  98.0 0.1 copy.20
  98.1 0.1 reshape.151
  98.2 0.1 iota_compare_fusion
  98.3 0.0 collective-permute-done
  98.3 0.0 collective-permute-done.1
  98.3 0.0 copy-done.3
  98.3 0.2 fusion.9
  98.6 1.0 gather_fusion.3
  99.6 0.1 bitcast_reduce_fusion
  99.7 18.8 %all-to-all-done = bf16[128,4,512]{2,1,0:T(4,128)(2,1)S(1)} async-done(((bf16[128,4,512]{2,1,0:T(4,128)(2,1)}), bf16[128,4,512]{2,1,0:T(4,128)(2,1)S(1)}, u32[]{:S(2)}, u32[]{:S(2)}) %all-to-all-start) | async-done | bytes 524320 | tf_op jit(solution)/shard_map/all_to_all | solution.py:66
  118.4 0.9 all_to_all.10
  119.4 1.8 fusion.4
  121.2 3.7 %gather_fusion.1 = f32[1536,128]{1,0:T(8,128)} fusion(f32[4608,128]{1,0:T(8,128)S(1)} %bitcast.41, s32[2048]{0:T(1024)S(1)} %pad_clamp_fusion), kind=kCustom, calls=%fused_computation.1 | custom fusion | bytes 1579008 | tf_op jit(solution)/shard_map/gather | solution.py:72
  124.9 1.5 select_reduce_fusion
  126.4 39.0 %all-gather.2.cloned.1.call-done = bf16[1024,512]{1,0:T(8,128)(2,1)} async-done(((bf16[8,512]{1,0:T(8,128)(2,1)}), bf16[1024,512]{1,0:T(8,128)(2,1)}) %all-gather.2.cloned.1.call-update) | async-done | bytes 1048592 | tf_op jit(solution)/shard_map/all_gather | solution.py:52
  165.4 2.4 %gather_fusion.2 = bf16[192,512]{1,0:T(8,128)(2,1)S(1)} fusion(bf16[1024,512]{1,0:T(8,128)(2,1)} %all-gather.2.cloned.1.call-done, s32[1024]{0:T(1024)S(1)} %pad_clamp_fusion.2), kind=kCustom, calls=%fused_computation.2 | custom fusion | bytes 393984 | tf_op jit(solution)/shard_map/gather | solution.py:53
  167.8 0.4 fusion.1
  168.3 8.4 %all_gather.17 = bf16[8,512]{1,0:T(8,128)(2,1)S(1)} all-gather(bf16[8,128]{1,0:T(8,128)(2,1)S(1)} %reduce_sum.28), channel_id=1, replica_groups=mesh['leaf'=128,'lvl'=4] {'lvl'}, dimensions={1}, use_global_device_ids=true | all-gather | bytes 10240 | tf_op jit(solution)/shard_map/all_gather | solution.py:61
  176.7 0.2 fusion.17
  176.9 8.2 %all_gather.18 = bf16[64,512]{1,0:T(8,128)(2,1)S(1)} all-gather(bf16[64,128]{1,0:T(8,128)(2,1)S(1)} %fusion.16), channel_id=1, replica_groups=mesh['leaf'=128,'lvl'=4] {'lvl'}, dimensions={1}, use_global_device_ids=true | all-gather | bytes 81920 | tf_op jit(solution)/shard_map/all_gather | solution.py:76
  185.1 1.7 convolution_add_fusion
  (18 shorter events, 0.1 us)
Async XLA Ops:
  6.5 112.8 %copy-start = (bf16[8,512,128]{2,1,0:T(8,128)(2,1)S(1)}, bf16[8,512,128]{2,1,0:T(8,128)(2,1)}, u32[]{:S(2)}) copy-start(bf16[8,512,128]{2,1,0:T(8,128)(2,1)} %param.19) | copy-start | bytes 3145732
  6.5 58.1 %all-reduce.2.cloned.1.call-start = ((), (), s32[]{:S(2)}) async-start(), calls=%async_computation.1 | async-start | bytes 131072 | tf_op jit(solution)/shard_map/psum | solution.py:46
  8.4 157.1 %all-gather.2.cloned.1.call-start = ((), (), s32[]{:S(2)}) async-start(), calls=%async_computation.2 | async-start | bytes 1056768 | tf_op jit(solution)/shard_map/all_gather | solution.py:52
  18.0 80.3 %collective-permute-start = (bf16[32,512]{1,0:T(8,128)(2,1)S(1)}, bf16[32,512]{1,0:T(8,128)(2,1)S(1)}, u32[]{:S(2)}, u32[]{:S(2)}) collective-permute-start(bf16[32,512]{1,0:T(8,128)(2,1)S(1)} %get-tuple-element.5), channel_id=1, source_target_pairs={{0,4},{4,8},{8,12},{12,16},{16,20},{20,24},{24,28},{28,32},{32,36}... | collective-permute-start | bytes 98312 | tf_op jit(solution)/shard_map/ppermute | solution.py:14
  24.4 73.9 %collective-permute-start.1 = (bf16[32,512]{1,0:T(8,128)(2,1)S(1)}, bf16[32,512]{1,0:T(8,128)(2,1)S(1)}, u32[]{:S(2)}, u32[]{:S(2)}) collective-permute-start(bf16[32,512]{1,0:T(8,128)(2,1)S(1)} %get-tuple-element.6), channel_id=1, source_target_pairs={{4,0},{8,4},{12,8},{16,12},{20,16},{24,20},{28,24},{32,28},{36,32}... | collective-permute-start | bytes 98312 | tf_op jit(solution)/shard_map/ppermute | solution.py:15
  64.7 11.4 %copy-start.1 = (bf16[64,512]{1,0:T(8,128)(2,1)S(1)}, bf16[64,512]{1,0:T(8,128)(2,1)}, u32[]{:S(2)}) copy-start(bf16[64,512]{1,0:T(8,128)(2,1)} %all-reduce.2.cloned.1.call-done) | copy-start | bytes 196612
  76.1 21.8 %copy-start.4 = (s32[8,24]{1,0:T(8,128)S(1)}, s32[8,24]{1,0:T(8,128)}, u32[]{:S(2)}) copy-start(s32[8,24]{1,0:T(8,128)} %param.29) | copy-start | bytes 2308
  76.1 22.0 %copy-start.5 = (s32[64]{0:T(128)S(1)}, s32[64]{0:T(128)}, u32[]{:S(2)}) copy-start(s32[64]{0:T(128)} %param.27) | copy-start | bytes 772
  76.2 22.2 %copy-start.3 = (bf16[4,512,128]{2,1,0:T(8,128)(2,1)S(1)}, bf16[4,512,128]{2,1,0:T(8,128)(2,1)}, u32[]{:S(2)}) copy-start(bf16[4,512,128]{2,1,0:T(8,128)(2,1)} %param.23) | copy-start | bytes 1572868
  79.1 39.4 %all-to-all-start = ((bf16[128,4,512]{2,1,0:T(4,128)(2,1)}), bf16[128,4,512]{2,1,0:T(4,128)(2,1)S(1)}, u32[]{:S(2)}, u32[]{:S(2)}) async-start(bf16[128,4,512]{2,1,0:T(4,128)(2,1)} %all_to_all.8), calls=%async_computation | async-start | bytes 1048576 | tf_op jit(solution)/shard_map/all_to_all | solution.py:66
  124.9 43.0 %copy-start.6 = (bf16[4,512,128]{2,1,0:T(8,128)(2,1)S(1)}, bf16[4,512,128]{2,1,0:T(8,128)(2,1)}, u32[]{:S(2)}) copy-start(bf16[4,512,128]{2,1,0:T(8,128)(2,1)} %param.20) | copy-start | bytes 1572868
  124.9 51.8 %copy-start.2 = (bf16[8,512,128]{2,1,0:T(8,128)(2,1)S(1)}, bf16[8,512,128]{2,1,0:T(8,128)(2,1)}, u32[]{:S(2)}) copy-start(bf16[8,512,128]{2,1,0:T(8,128)(2,1)} %param.21) | copy-start | bytes 3145732
Sparse Core Ops, SparseCore 0:
  9.7 54.9 all-reduce.1
  74.8 90.5 all-gather.1
where the time goes:
time: 197 us; the launch traced here: 194 us
  waiting for transfers between devices  91.6 us (46%)
  blocking collectives  34.5 us (18%)
  starting transfers between devices  29.9 us (15%)
  between operations  13.6 us (7%)
  local copies, waits for them, and re-layouts  13.1 us (7%)
  matrix products  7.72 us (4%)
  other arithmetic  3.21 us (2%)
    all_gather x1, waiting for transfers between devices, local(): coarse_all = lax.all_gather(parents, 'leaf', axis=0, tiled=True)  39 us
    psum x1, waiting for transfers between devices, local(): moments = lax.psum(partial_value.astype(jnp.bfloat16), 'lvl')  33.8 us
    all_to_all x1, waiting for transfers between devices, local(): lax.all_to_all(outgoing, 'leaf', split_axis=0, concat_axis=0, tiled=True)  18.8 us
    all_to_all x1, starting transfers between devices, local(): lax.all_to_all(outgoing, 'leaf', split_axis=0, concat_axis=0, tiled=True)  18.6 us
    all_gather x1, blocking collectives, local(): all_points = lax.all_gather(charges, 'lvl', axis=1, tiled=True)  9.55 us
    all_gather x1, blocking collectives, local(): parents = lax.all_gather(parent_part, 'lvl', axis=1, tiled=True)  8.41 us
    all_gather x1, blocking collectives, local(): parent_local = lax.all_gather(coarse_part, 'lvl', axis=1, tiled=True)  8.38 us
    all_gather x1, blocking collectives, local(): local_full = lax.all_gather(local_part, 'lvl', axis=1, tiled=True)  8.16 us
  transfers between devices with their start and end apart: 5, of which 3 were waited for; matrix products, arithmetic and copies ran while one was open for 8% of the time, Pallas kernels for 0%

commit v1 on v0

v1 whole, which is shorter than its diff:
```python
import jax
import jax.numpy as jnp
from jax import lax
from jax.experimental import pallas as pl
from jax.experimental.pallas import tpu as pltpu
from jax.sharding import PartitionSpec as P

MESH = pl.DeviceIdType.MESH
BF16 = jnp.bfloat16
F32 = jnp.float32
I32 = jnp.int32
XOFF = (2, 1, 3)


def mm(a, b):
    return jnp.dot(a, b, preferred_element_type=F32)


def mm_nt(a, b):
    return lax.dot_general(a, b, (((1,), (1,)), ((), ())), preferred_element_type=F32)


def iota(shape, dim):
    return lax.broadcasted_iota(I32, shape, dim)


def flipped(code):
    slots, leaves = code.shape
    halves = jnp.concatenate([code >> 6, code & 63], axis=0).astype(F32).astype(BF16)
    eye = (iota((leaves, leaves), 0) == iota((leaves, leaves), 1)).astype(F32).astype(BF16)
    turned = mm_nt(eye, halves)
    return (turned[:, :slots] * 64.0 + turned[:, slots:]).astype(I32)


def counts(code, width, start):
    rows, slots = code.shape
    columns = iota((rows, width), 1)
    code = code - start
    total = jnp.zeros((rows, width), F32)
    for s in range(slots):
        total = total + jnp.where(code[:, s : s + 1] == columns, 1.0, 0.0)
    return total.astype(BF16)


def kernel(
    charges_h, p2m_h, m2m_h, lops_h, cops_h, l2l_h, l2p_h, tiles_h,
    send_h, src_h, op_h, count_h, csrc_h, cop_h, near_h, kind_h,
    out_ref,
    charges, p2m, m2m, l2l, l2p, tiles,
    send, src, op, count, csrc, cop, near_v, kind_v,
    load_sem,
    mom32, mom4, mpart, mslot, ext, leafw, coarsew,
    pick, s_leaf, s_coarse, s_near,
    msg, rbuf, cbuf, pool, gsum,
    coarse_own, coarse_slot, down, leafpot, pot, pot_out, pot_slot,
    mp_s, mp_r, ch_s, ch_r, lw_s, lw_r, cw_s, cw_r, own_w, sw_s, sw_r,
    halo_s, halo_r, far_s, far_r, sib_s, sib_r, co_s, co_r, po_s, po_r,
    ready,
):
    leaf = lax.axis_index("leaf")
    lvl = lax.axis_index("lvl")
    core = lax.rem(leaf, 2)
    chip = lax.div(leaf, 2)
    z = lax.div(leaf, 16)
    y = lax.rem(chip, 8)
    other = 1 - core
    sibling = (chip * 2 + other, lvl)
    right = (lax.rem(leaf + 1, 128), lvl)
    left = (lax.rem(leaf + 127, 128), lvl)
    beside = (lax.rem(leaf + 127 + 2 * core, 128), lvl)
    near_far = (4, 3, 5, 2, 6, 1, 7)
    zpeers = [(lax.rem(z + k, 8) * 16 + y * 2 + core, lvl) for k in near_far]
    ypeers = [(z * 16 + lax.rem(y + k, 8) * 2 + core, lvl) for k in near_far]
    xpeers = [(leaf, lax.rem(lvl + k, 4)) for k in XOFF]
    mine = pl.ds(pl.multiple_of(lvl * 128, 128), 128)

    barrier = pltpu.get_barrier_semaphore()
    greeted = zpeers + ypeers + xpeers + [sibling, beside]
    for peer in greeted:
        pl.semaphore_signal(barrier, inc=1, device_id=peer, device_id_type=MESH)

    loads = {}
    pairs = (
        ("charges", charges_h, charges), ("p2m", p2m_h, p2m), ("send", send_h, send),
        ("csrc", csrc_h, csrc), ("cop", cop_h, cop), ("near", near_h, near_v), ("kind", kind_h, kind_v),
        ("src", src_h, src), ("op", op_h, op), ("count", count_h, count),
        ("m2m", m2m_h, m2m), ("tiles", tiles_h, tiles), ("l2l", l2l_h, l2l), ("l2p", l2p_h, l2p),
    )
    for i, (name, source, target) in enumerate(pairs):
        loads[name] = pltpu.make_async_copy(source, target, load_sem.at[i])
        loads[name].start()

    def remote(source, target, send_sem, recv_sem, peer):
        copy = pltpu.make_async_remote_copy(
            src_ref=source, dst_ref=target, send_sem=send_sem, recv_sem=recv_sem,
            device_id=peer, device_id_type=MESH,
        )
        copy.start()
        return copy

    loads["charges"].wait()
    loads["p2m"].wait()
    partial = mm(charges[...], p2m[...])
    mom32[...] = partial
    mpart[...] = partial.astype(BF16)
    ext[32:96, mine] = charges[...]

    loads["send"].wait()
    row = iota((512, 128), 0)
    dest = (row >> 3) * 2 + jnp.where(((row >> 2) & 1) == 0, core, other)
    spread = (dest == iota((512, 128), 1)).astype(F32).astype(BF16)
    chosen = mm_nt(spread, send[...].astype(F32).astype(BF16))
    slot = iota((512, 4), 1) == (iota((512, 4), 0) & 3)
    chosen = jnp.sum(jnp.where(slot, chosen, 0.0), axis=1, keepdims=True).astype(I32)
    pick[...] = (chosen == iota((512, 64), 1)).astype(F32).astype(BF16)

    loads["csrc"].wait()
    loads["cop"].wait()
    cv = csrc[...]
    cpos = (cv & ~15) + (cv & 7) + jnp.where(((cv >> 3) & 1) == core, 0, 1024)
    ctag = cop[...]
    ccode = jnp.concatenate([jnp.where(ctag == t, cpos, -1) for t in range(4)], axis=0)
    for part in range(4):
        s_coarse[:, part * 512 : (part + 1) * 512] = counts(ccode, 512, part * 512)

    loads["near"].wait()
    loads["kind"].wait()
    ncode = kind_v[...] * 128 + (near_v[...] - (leaf * 64 - 32))
    s_near[...] = counts(flipped(ncode), 512, 0)

    pl.semaphore_wait(barrier, len(greeted))

    mp = [remote(mpart, mslot.at[i], mp_s.at[i], mp_r.at[i], xpeers[i]) for i in range(3)]
    ch = [
        remote(charges, ext.at[pl.ds(32, 64), mine], ch_s.at[i], ch_r.at[i], xpeers[i])
        for i in range(3)
    ]
    for peer in ypeers:
        pl.semaphore_signal(ready, inc=1, device_id=peer, device_id_type=MESH)

    loads["src"].wait()
    loads["op"].wait()
    loads["count"].wait()
    sv = src[...]
    w = sv - 64
    sent = 64 + ((w >> 3) << 2) + (w & 3) + jnp.where(((w >> 2) & 1) == core, 0, 256)
    spos = jnp.where(sv < 64, sv, sent)
    scode = jnp.where(iota((24, 64), 0) < count[...], op[...] * 640 + spos, -1)
    scode = flipped(scode)

    def fill(t, carry):
        s_leaf[:, pl.ds(pl.multiple_of(t * 640, 128), 640)] = counts(scode, 640, t * 640)
        return carry

    lax.fori_loop(0, 8, fill, 0)

    for copy in mp:
        copy.wait_recv()
    moments = mom32[...]
    for i in range(3):
        moments = moments + mslot[i].astype(F32)
    moments = moments.astype(BF16).astype(F32)
    for j in range(4):
        mom4[j] = moments[:, j * 128 : (j + 1) * 128]

    chalf = pl.ds(core * 2, 2)
    lhalf = pl.ds(core * 4, 4)
    cw, lw = [], []
    for i, k in enumerate(XOFF):
        rows = pl.ds(pl.multiple_of(lax.rem(lvl + k, 4) * 128, 128), 128)
        cw.append(remote(cops_h.at[chalf, rows], coarsew.at[chalf, :, mine], cw_s.at[i], cw_r.at[i], xpeers[i]))
    for i, k in enumerate(XOFF):
        rows = pl.ds(pl.multiple_of(lax.rem(lvl + k, 4) * 128, 128), 128)
        lw.append(remote(lops_h.at[lhalf, rows], leafw.at[lhalf, :, mine], lw_s.at[i], lw_r.at[i], xpeers[i]))
    own_c = pltpu.make_async_copy(cops_h.at[chalf, mine], coarsew.at[chalf, :, mine], own_w.at[0])
    own_l = pltpu.make_async_copy(lops_h.at[lhalf, mine], leafw.at[lhalf, :, mine], own_w.at[1])
    own_c.start()
    own_l.start()

    loads["m2m"].wait()
    parents = jnp.zeros((8, 128), F32)
    for o in range(8):
        octant = [mom4[j, pl.ds(o, 8, stride=8), :] for j in range(4)]
        parents = parents + mm(jnp.concatenate(octant, axis=1).astype(BF16), m2m[o])
    quarter = mom4[lvl].astype(BF16)
    chosen_rows = mm(pick[...], quarter).reshape(64, 8, 128)
    both = jnp.concatenate([jnp.broadcast_to(parents[None], (64, 8, 128)), chosen_rows], axis=1)
    msg[...] = both.astype(BF16)

    pl.semaphore_wait(ready, 7)

    def offset(t):
        return 4 + (1 - 2 * lax.rem(t, 2)) * lax.div(t + 1, 2)

    def send_one(i, carry):
        pz = lax.rem(z + offset(lax.div(i, 8)), 8)
        py = lax.rem(y + offset(lax.rem(i, 8)), 8)
        there = pz * 8 + py
        pltpu.make_async_remote_copy(
            src_ref=msg.at[there], dst_ref=rbuf.at[chip], send_sem=far_s, recv_sem=far_r,
            device_id=(there * 2 + core, lvl), device_id_type=MESH,
        ).start()
        return carry

    lax.fori_loop(0, 63, send_one, 0)
    rbuf[pl.ds(chip, 1)] = msg[pl.ds(chip, 1)]
    pool[0:64, :] = quarter
    pool[576:640, :] = jnp.zeros((64, 128), BF16)

    for copy in ch:
        copy.wait_recv()
    halo = [
        remote(ext.at[pl.ds(64, 32)], ext.at[pl.ds(0, 32)], halo_s.at[0], halo_r.at[0], right),
        remote(ext.at[pl.ds(32, 32)], ext.at[pl.ds(96, 32)], halo_s.at[1], halo_r.at[1], left),
    ]

    own_c.wait()
    for copy in cw:
        copy.wait_recv()
    swap = [remote(coarsew.at[chalf], coarsew.at[chalf], sw_s.at[0], sw_r.at[0], sibling)]

    for copy in halo:
        copy.wait_recv()
    loads["tiles"].wait()
    close = jnp.zeros((64, 128), F32)
    for t in range(4):
        close = close + mm(s_near[:, t * 128 : (t + 1) * 128], mm(ext[...], tiles[t]).astype(BF16))
    out_ref[...] = close

    own_l.wait()
    for copy in lw:
        copy.wait_recv()
    swap.append(remote(leafw.at[lhalf], leafw.at[lhalf], sw_s.at[1], sw_r.at[1], sibling))

    pltpu.make_async_copy(msg.at[pl.ds(0, 63)], rbuf.at[pl.ds(0, 63)], far_r).wait()
    sib = remote(rbuf, cbuf, sib_s, sib_r, sibling)
    gathered = mm(s_coarse[:, :1024], rbuf[...].reshape(1024, 128))

    def swapped(x):
        return jnp.concatenate([x[:, 4:], x[:, :4]], axis=1)

    low = iota((32, 8, 128), 1) < 4
    pairs_own = rbuf[...].astype(F32)[:, 8:].reshape(32, 2, 8, 128)
    own_rows = jnp.where(low, pairs_own[:, 0], swapped(pairs_own[:, 1]))
    pool[64:320, :] = own_rows.reshape(256, 128).astype(BF16)
    swap[0].wait_recv()
    sib.wait_recv()

    gathered = gathered + mm(s_coarse[:, 1024:], cbuf[...].reshape(1024, 128))
    gathered = gathered.astype(BF16)
    coarse = jnp.zeros((8, 512), F32)
    for t in range(4):
        coarse = coarse + mm(gathered[t * 8 : (t + 1) * 8], coarsew[t])
    coarse_own[...] = coarse
    co = [remote(coarse_own, coarse_slot.at[i], co_s.at[i], co_r.at[i], xpeers[i]) for i in range(3)]

    pairs_sib = cbuf[...].astype(F32)[:, 8:].reshape(32, 2, 8, 128)
    sib_rows = jnp.where(low, swapped(pairs_sib[:, 0]), pairs_sib[:, 1])
    pool[320:576, :] = sib_rows.reshape(256, 128).astype(BF16)
    for t in range(8):
        gsum[:, t * 128 : (t + 1) * 128] = mm(s_leaf[:, t * 640 : (t + 1) * 640], pool[...]).astype(BF16)
    swap[1].wait_recv()
    far = mm(gsum[...], leafw[...].reshape(1024, 512)).astype(BF16)
    loads["l2p"].wait()
    leafpot[...] = mm(far, l2p[...])

    loads["l2l"].wait()
    for copy in co:
        copy.wait_recv()
    coarse = coarse_own[...]
    for i in range(3):
        coarse = coarse + coarse_slot[i]
    coarse = coarse.astype(BF16)
    for o in range(8):
        down[pl.ds(o, 8, stride=8), :] = mm(coarse, l2l[o])
    pot[...] = leafpot[...] + mm(down[...].astype(BF16), l2p[mine, :])
    for j in range(4):
        pot_out[j] = pot[:, j * 128 : (j + 1) * 128].astype(BF16)
    po = [
        remote(pot_out.at[lax.rem(lvl + k, 4)], pot_slot.at[i], po_s.at[i], po_r.at[i], xpeers[i])
        for i, k in enumerate(XOFF)
    ]
    result = out_ref[...] + pot[:, mine]

    for copy in mp + ch + cw + lw + swap + halo + [sib] + co:
        copy.wait_send()
    pltpu.make_async_copy(msg.at[pl.ds(0, 63)], rbuf.at[pl.ds(0, 63)], far_s).wait()
    for copy in po:
        copy.wait_recv()
    for i in range(3):
        result = result + pot_slot[i].astype(F32)
    out_ref[...] = result
    for copy in po:
        copy.wait_send()


def local(
    charges, p2m_matrix, m2m_matrices, leaf_ops, coarse_ops, l2l_matrices, l2p_matrix, near_kernel_tiles,
    send_rows, m2l_src, m2l_op, m2l_count, coarse_src, coarse_op, near_src, neighbour_kernel_type,
):
    operands = (
        charges, p2m_matrix, m2m_matrices, leaf_ops, coarse_ops, l2l_matrices, l2p_matrix, near_kernel_tiles,
        jnp.swapaxes(send_rows, 1, 2).reshape(4, 128), m2l_src.T, m2l_op.T, m2l_count.reshape(1, 64),
        coarse_src, coarse_op, near_src.T, neighbour_kernel_type.T,
    )
    dma = pltpu.SemaphoreType.DMA
    vmem = pltpu.VMEM
    scratch = [
        vmem((64, 128), BF16), vmem((128, 512), BF16), vmem((8, 512, 128), BF16), vmem((8, 512, 128), BF16),
        vmem((512, 512), BF16), vmem((4, 512, 128), BF16),
        vmem((4, 128), I32), vmem((24, 64), I32), vmem((24, 64), I32), vmem((1, 64), I32),
        vmem((8, 24), I32), vmem((8, 24), I32), vmem((8, 64), I32), vmem((8, 64), I32),
        dma((14,)),
        vmem((64, 512), F32), vmem((4, 64, 128), F32), vmem((64, 512), BF16), vmem((3, 64, 512), BF16), vmem((128, 512), BF16),
        vmem((8, 128, 512), BF16), vmem((4, 128, 512), BF16),
        vmem((512, 64), BF16), vmem((64, 5120), BF16), vmem((32, 2048), BF16), vmem((64, 512), BF16),
        vmem((64, 16, 128), BF16), vmem((64, 16, 128), BF16), vmem((64, 16, 128), BF16),
        vmem((640, 128), BF16), vmem((64, 1024), BF16),
        vmem((8, 512), F32), vmem((3, 8, 512), F32), vmem((64, 128), F32), vmem((64, 512), F32),
        vmem((64, 512), F32), vmem((4, 64, 128), BF16), vmem((3, 64, 128), BF16),
        dma((3,)), dma((3,)), dma((3,)), dma((3,)), dma((3,)), dma((3,)), dma((3,)), dma((3,)),
        dma((2,)), dma((2,)), dma((2,)), dma((2,)), dma((2,)),
        dma, dma, dma, dma, dma((3,)), dma((3,)), dma((3,)), dma((3,)),
        pltpu.SemaphoreType.REGULAR,
    ]
    return pl.pallas_call(
        kernel,
        out_shape=jax.ShapeDtypeStruct((64, 128), F32),
        in_specs=[pl.BlockSpec(memory_space=pl.ANY)] * len(operands),
        out_specs=pl.BlockSpec(memory_space=pltpu.VMEM),
        scratch_shapes=scratch,
        compiler_params=pltpu.CompilerParams(
            collective_id=0, has_side_effects=True, vmem_limit_bytes=60 * 2**20
        ),
    )(*operands)


def solution(mesh):
    placed = (
        P("leaf", "lvl"),
        P("lvl", None),
        P(None, None, "lvl"),
        P(None, None, "lvl"),
        P(None, None, "lvl"),
        P(None, None, "lvl"),
        P(),
        P(None, None, "lvl"),
        P("leaf", None, None),
        P("leaf", None),
        P("leaf", None),
        P("leaf"),
        P("leaf", None),
        P("leaf", None),
        P("leaf", None),
        P("leaf", None),
    )
    return jax.shard_map(
        local, mesh=mesh, in_specs=placed, out_specs=P("leaf", "lvl"), check_vma=False
    )
```

time: 197 us -> 41.8 us (0.21); the launches traced: 194 us -> 41.6 us
  waiting for transfers between devices: 91.6 us -> 0 us
  Pallas kernels: 0 us -> 40.2 us
  blocking collectives: 34.5 us -> 0 us
  starting transfers between devices: 29.9 us -> 0 us
  between operations: 13.6 us -> 0.01 us
  local copies, waits for them, and re-layouts: 13.1 us -> 1.38 us
  matrix products: 7.72 us -> 0 us
  other arithmetic: 3.21 us -> 0 us
    pallas_call x0 -> x1, Pallas kernels: none -> 40.2 us  [local(): pl.pallas_call(kernel, out_shape=jax.ShapeDtypeStruct((64, 128), F32), in...]
    all_gather x1 -> x0, waiting for transfers between devices: 39 us -> none  [local(): coarse_all = lax.all_gather(parents, 'leaf', axis=0, tiled=True)]
    all_gather x4 -> x0, blocking collectives: 34.5 us -> none  [the longest x1 9.55 us: local(): all_points = lax.all_gather(charges, 'lvl', axis=1, tiled=True)]
    psum x1 -> x0, waiting for transfers between devices: 33.8 us -> none  [local(): moments = lax.psum(partial_value.astype(jnp.bfloat16), 'lvl')]
    all_to_all x1 -> x0, waiting for transfers between devices: 18.8 us -> none  [local(): lax.all_to_all(outgoing, 'leaf', split_axis=0, concat_axis=0, tiled=True)]
    all_to_all x1 -> x0, starting transfers between devices: 18.6 us -> none  [local(): lax.all_to_all(outgoing, 'leaf', split_axis=0, concat_axis=0, tiled=True)]
    ppermute x2 -> x0, starting transfers between devices: 11.2 us -> none  [the longest x1 6.39 us: with_halo(): before = lax.ppermute(last, axis, up)]
    gather x4 -> x0, local copies, waits for them, and re-layouts: 9.1 us -> none  [the longest x1 3.69 us: local(): picked = flat_table[flat_index]]
  transfers between devices with their start and end apart: 5 -> 0, of which waited for: 3 -> 0; matrix products, arithmetic and copies ran while one was open for 8% -> 0% of each run, Pallas kernels for 0% -> 0%
where the time goes in v1:
time: 41.8 us; the launch traced here: 41.6 us
  Pallas kernels  40.2 us (96%)
  local copies, waits for them, and re-layouts  1.38 us (3%)
    pallas_call x1, Pallas kernels, local(): pl.pallas_call(kernel, out_shape=jax.ShapeDtypeStruct((64, 128), F32), in...  40.2 us
    unnamed x1, local copies, waits for them, and re-layouts  1.38 us

profile of v1, /device:TPU:1, one launch (start us, length us, event | category | flops | bytes accessed | tf_op | source)
XLA Modules:
  0.0 41.6 jit_solution(16779420348745604561)
XLA Ops:
  0.0 40.2 %shard_map.154 = f32[64,128]{1,0:T(8,128)} custom-call(bf16[64,128]{1,0:T(8,128)(2,1)} %charges_h.1, bf16[128,512]{1,0:T(8,128)(2,1)} %p2m_h.1, bf16[8,512,128]{2,1,0:T(8,128)(2,1)} %m2m_h.1, bf16[8,512,128]{2,1,0:T(8,128)(2,1)} %lops_h.1, bf16[4,512,128]{2,1,0:T(8,128)(2,1)} %cops_h.1, bf16[8,512,128]{2,1,0:T(8,128)(2,1)} %l2l_h.1, bf16[512,512]{1,0:T(8,128)(2,1)} %l2p_h.1, ...), custom_call_target="tpu_custom_call" | custom-call | tf_op jit(solution)/shard_map/pallas_call | solution.py:326
  40.2 1.4 %copy.18 = f32[64,128]{1,0:T(8,128)} copy(f32[64,128]{1,0:T(8,128)} %shard_map.154) | data formatting | bytes 65536

commit v2 on v1

--- a/solution.py
+++ b/solution.py
@@ -47,15 +47,15 @@
     send_h, src_h, op_h, count_h, csrc_h, cop_h, near_h, kind_h,
     out_ref,
     charges, p2m, m2m, l2l, l2p, tiles,
-    send, src, op, count, csrc, cop, near_v, kind_v,
+    send, src, op, count, cells, near_v, kind_v,
     load_sem,
     mom32, mom4, mpart, mslot, ext, leafw, coarsew,
     pick, s_leaf, s_coarse, s_near,
-    msg, rbuf, cbuf, pool, gsum,
+    msg, rbuf, cbuf, pool,
     coarse_own, coarse_slot, down, leafpot, pot, pot_out, pot_slot,
     mp_s, mp_r, ch_s, ch_r, lw_s, lw_r, cw_s, cw_r, own_w, sw_s, sw_r,
     halo_s, halo_r, far_s, far_r, sib_s, sib_r, co_s, co_r, po_s, po_r,
-    ready,
+    ct_s, ct_r, ready,
 ):
     leaf = lax.axis_index("leaf")
     lvl = lax.axis_index("lvl")
@@ -72,17 +72,18 @@
     zpeers = [(lax.rem(z + k, 8) * 16 + y * 2 + core, lvl) for k in near_far]
     ypeers = [(z * 16 + lax.rem(y + k, 8) * 2 + core, lvl) for k in near_far]
     xpeers = [(leaf, lax.rem(lvl + k, 4)) for k in XOFF]
+    across = [(chip * 2 + other, lax.rem(lvl + k, 4)) for k in XOFF]
     mine = pl.ds(pl.multiple_of(lvl * 128, 128), 128)
 
     barrier = pltpu.get_barrier_semaphore()
-    greeted = zpeers + ypeers + xpeers + [sibling, beside]
+    greeted = zpeers + ypeers + xpeers + across + [sibling, beside]
     for peer in greeted:
         pl.semaphore_signal(barrier, inc=1, device_id=peer, device_id_type=MESH)
 
     loads = {}
     pairs = (
         ("charges", charges_h, charges), ("p2m", p2m_h, p2m), ("send", send_h, send),
-        ("csrc", csrc_h, csrc), ("cop", cop_h, cop), ("near", near_h, near_v), ("kind", kind_h, kind_v),
+        ("csrc", csrc_h, cells.at[0, 0]), ("cop", cop_h, cells.at[0, 1]), ("near", near_h, near_v), ("kind", kind_h, kind_v),
         ("src", src_h, src), ("op", op_h, op), ("count", count_h, count),
         ("m2m", m2m_h, m2m), ("tiles", tiles_h, tiles), ("l2l", l2l_h, l2l), ("l2p", l2p_h, l2p),
     )
@@ -104,6 +105,19 @@
     mom32[...] = partial
     mpart[...] = partial.astype(BF16)
     ext[32:96, mine] = charges[...]
+
+    pl.semaphore_wait(barrier, len(greeted))
+
+    mp = [remote(mpart, mslot.at[i], mp_s.at[i], mp_r.at[i], xpeers[i]) for i in range(3)]
+    ch = [
+        remote(charges, ext.at[pl.ds(32, 64), mine], ch_s.at[i], ch_r.at[i], xpeers[i])
+        for i in range(3)
+    ]
+    loads["csrc"].wait()
+    loads["cop"].wait()
+    ct = [remote(cells.at[0], cells.at[1], ct_s, ct_r, sibling)]
+    for peer in ypeers:
+        pl.semaphore_signal(ready, inc=1, device_id=peer, device_id_type=MESH)
 
     loads["send"].wait()
     row = iota((512, 128), 0)
@@ -114,42 +128,18 @@
     chosen = jnp.sum(jnp.where(slot, chosen, 0.0), axis=1, keepdims=True).astype(I32)
     pick[...] = (chosen == iota((512, 64), 1)).astype(F32).astype(BF16)
 
-    loads["csrc"].wait()
-    loads["cop"].wait()
-    cv = csrc[...]
-    cpos = (cv & ~15) + (cv & 7) + jnp.where(((cv >> 3) & 1) == core, 0, 1024)
-    ctag = cop[...]
-    ccode = jnp.concatenate([jnp.where(ctag == t, cpos, -1) for t in range(4)], axis=0)
-    for part in range(4):
-        s_coarse[:, part * 512 : (part + 1) * 512] = counts(ccode, 512, part * 512)
-
-    loads["near"].wait()
-    loads["kind"].wait()
-    ncode = kind_v[...] * 128 + (near_v[...] - (leaf * 64 - 32))
-    s_near[...] = counts(flipped(ncode), 512, 0)
-
-    pl.semaphore_wait(barrier, len(greeted))
-
-    mp = [remote(mpart, mslot.at[i], mp_s.at[i], mp_r.at[i], xpeers[i]) for i in range(3)]
-    ch = [
-        remote(charges, ext.at[pl.ds(32, 64), mine], ch_s.at[i], ch_r.at[i], xpeers[i])
-        for i in range(3)
-    ]
-    for peer in ypeers:
-        pl.semaphore_signal(ready, inc=1, device_id=peer, device_id_type=MESH)
-
     loads["src"].wait()
     loads["op"].wait()
     loads["count"].wait()
     sv = src[...]
     w = sv - 64
-    sent = 64 + ((w >> 3) << 2) + (w & 3) + jnp.where(((w >> 2) & 1) == core, 0, 256)
-    spos = jnp.where(sv < 64, sv, sent)
+    sent = ((w >> 3) << 2) + (w & 3) + jnp.where(((w >> 2) & 1) == core, 0, 256)
+    spos = jnp.where(sv < 64, sv + 512, sent)
     scode = jnp.where(iota((24, 64), 0) < count[...], op[...] * 640 + spos, -1)
     scode = flipped(scode)
 
     def fill(t, carry):
-        s_leaf[:, pl.ds(pl.multiple_of(t * 640, 128), 640)] = counts(scode, 640, t * 640)
+        s_leaf[pl.ds(pl.multiple_of(t * 64, 64), 64), :] = counts(scode, 640, t * 640)
         return carry
 
     lax.fori_loop(0, 8, fill, 0)
@@ -204,8 +194,24 @@
 
     lax.fori_loop(0, 63, send_one, 0)
     rbuf[pl.ds(chip, 1)] = msg[pl.ds(chip, 1)]
-    pool[0:64, :] = quarter
+    pool[512:576, :] = quarter
     pool[576:640, :] = jnp.zeros((64, 128), BF16)
+
+    for copy in ct:
+        copy.wait_recv()
+    ccode = []
+    for c in range(2):
+        cv = cells[c, 0]
+        cpos = jnp.where(((cv >> 3) & 1) == core, (cv & ~15) + (cv & 7), -1)
+        ccode += [jnp.where(cells[c, 1] == t, cpos, -1) for t in range(4)]
+    ccode = jnp.concatenate(ccode, axis=0)
+    for part in range(2):
+        s_coarse[:, part * 512 : (part + 1) * 512] = counts(ccode, 512, part * 512)
+
+    loads["near"].wait()
+    loads["kind"].wait()
+    ncode = kind_v[...] * 128 + (near_v[...] - (leaf * 64 - 32))
+    s_near[...] = counts(flipped(ncode), 512, 0)
 
     for copy in ch:
         copy.wait_recv()
@@ -234,7 +240,16 @@
 
     pltpu.make_async_copy(msg.at[pl.ds(0, 63)], rbuf.at[pl.ds(0, 63)], far_r).wait()
     sib = remote(rbuf, cbuf, sib_s, sib_r, sibling)
-    gathered = mm(s_coarse[:, :1024], rbuf[...].reshape(1024, 128))
+    gathered = mm(s_coarse[...], rbuf[...].reshape(1024, 128)).astype(BF16)
+    swap[0].wait_recv()
+    coarse = jnp.zeros((16, 512), F32)
+    for t in range(4):
+        rows = jnp.concatenate([gathered[t * 8 : t * 8 + 8], gathered[32 + t * 8 : 40 + t * 8]], axis=0)
+        coarse = coarse + mm(rows, coarsew[t])
+    coarse_own[...] = coarse.reshape(2, 8, 512)
+    co = [remote(coarse_own.at[0], coarse_slot.at[i], co_s.at[i], co_r.at[i], xpeers[i]) for i in range(3)]
+    co += [remote(coarse_own.at[1], coarse_slot.at[3 + i], co_s.at[3 + i], co_r.at[3 + i], across[i]) for i in range(3)]
+    co += [remote(coarse_own.at[1], coarse_slot.at[6], co_s.at[6], co_r.at[6], sibling)]
 
     def swapped(x):
         return jnp.concatenate([x[:, 4:], x[:, :4]], axis=1)
@@ -242,33 +257,25 @@
     low = iota((32, 8, 128), 1) < 4
     pairs_own = rbuf[...].astype(F32)[:, 8:].reshape(32, 2, 8, 128)
     own_rows = jnp.where(low, pairs_own[:, 0], swapped(pairs_own[:, 1]))
-    pool[64:320, :] = own_rows.reshape(256, 128).astype(BF16)
-    swap[0].wait_recv()
+    pool[0:256, :] = own_rows.reshape(256, 128).astype(BF16)
+    picked = mm(s_leaf[:, 0:256], pool[0:256, :]) + mm(s_leaf[:, 512:640], pool[512:640, :])
     sib.wait_recv()
-
-    gathered = gathered + mm(s_coarse[:, 1024:], cbuf[...].reshape(1024, 128))
-    gathered = gathered.astype(BF16)
-    coarse = jnp.zeros((8, 512), F32)
-    for t in range(4):
-        coarse = coarse + mm(gathered[t * 8 : (t + 1) * 8], coarsew[t])
-    coarse_own[...] = coarse
-    co = [remote(coarse_own, coarse_slot.at[i], co_s.at[i], co_r.at[i], xpeers[i]) for i in range(3)]
 
     pairs_sib = cbuf[...].astype(F32)[:, 8:].reshape(32, 2, 8, 128)
     sib_rows = jnp.where(low, swapped(pairs_sib[:, 0]), pairs_sib[:, 1])
-    pool[320:576, :] = sib_rows.reshape(256, 128).astype(BF16)
-    for t in range(8):
-        gsum[:, t * 128 : (t + 1) * 128] = mm(s_leaf[:, t * 640 : (t + 1) * 640], pool[...]).astype(BF16)
+    pool[256:512, :] = sib_rows.reshape(256, 128).astype(BF16)
+    picked = (picked + mm(s_leaf[:, 256:512], pool[256:512, :])).astype(BF16)
+    picked = jnp.concatenate([picked[t * 64 : (t + 1) * 64] for t in range(8)], axis=1)
     swap[1].wait_recv()
-    far = mm(gsum[...], leafw[...].reshape(1024, 512)).astype(BF16)
+    far = mm(picked, leafw[...].reshape(1024, 512)).astype(BF16)
     loads["l2p"].wait()
     leafpot[...] = mm(far, l2p[...])
 
     loads["l2l"].wait()
     for copy in co:
         copy.wait_recv()
-    coarse = coarse_own[...]
-    for i in range(3):
+    coarse = coarse_own[0]
+    for i in range(7):
         coarse = coarse + coarse_slot[i]
     coarse = coarse.astype(BF16)
     for o in range(8):
@@ -282,7 +289,7 @@
     ]
     result = out_ref[...] + pot[:, mine]
 
-    for copy in mp + ch + cw + lw + swap + halo + [sib] + co:
+    for copy in ct + mp + ch + cw + lw + swap + halo + [sib] + co:
         copy.wait_send()
     pltpu.make_async_copy(msg.at[pl.ds(0, 63)], rbuf.at[pl.ds(0, 63)], far_s).wait()
     for copy in po:
@@ -309,19 +316,19 @@
         vmem((64, 128), BF16), vmem((128, 512), BF16), vmem((8, 512, 128), BF16), vmem((8, 512, 128), BF16),
         vmem((512, 512), BF16), vmem((4, 512, 128), BF16),
         vmem((4, 128), I32), vmem((24, 64), I32), vmem((24, 64), I32), vmem((1, 64), I32),
-        vmem((8, 24), I32), vmem((8, 24), I32), vmem((8, 64), I32), vmem((8, 64), I32),
+        vmem((2, 2, 8, 24), I32), vmem((8, 64), I32), vmem((8, 64), I32),
         dma((14,)),
         vmem((64, 512), F32), vmem((4, 64, 128), F32), vmem((64, 512), BF16), vmem((3, 64, 512), BF16), vmem((128, 512), BF16),
         vmem((8, 128, 512), BF16), vmem((4, 128, 512), BF16),
-        vmem((512, 64), BF16), vmem((64, 5120), BF16), vmem((32, 2048), BF16), vmem((64, 512), BF16),
+        vmem((512, 64), BF16), vmem((512, 640), BF16), vmem((64, 1024), BF16), vmem((64, 512), BF16),
         vmem((64, 16, 128), BF16), vmem((64, 16, 128), BF16), vmem((64, 16, 128), BF16),
-        vmem((640, 128), BF16), vmem((64, 1024), BF16),
-        vmem((8, 512), F32), vmem((3, 8, 512), F32), vmem((64, 128), F32), vmem((64, 512), F32),
+        vmem((640, 128), BF16),
+        vmem((2, 8, 512), F32), vmem((7, 8, 512), F32), vmem((64, 128), F32), vmem((64, 512), F32),
         vmem((64, 512), F32), vmem((4, 64, 128), BF16), vmem((3, 64, 128), BF16),
         dma((3,)), dma((3,)), dma((3,)), dma((3,)), dma((3,)), dma((3,)), dma((3,)), dma((3,)),
         dma((2,)), dma((2,)), dma((2,)), dma((2,)), dma((2,)),
-        dma, dma, dma, dma, dma((3,)), dma((3,)), dma((3,)), dma((3,)),
-        pltpu.SemaphoreType.REGULAR,
+        dma, dma, dma, dma, dma((7,)), dma((7,)), dma((3,)), dma((3,)),
+        dma, dma, pltpu.SemaphoreType.REGULAR,
     ]
     return pl.pallas_call(
         kernel,

time: 41.8 us -> 40.5 us (0.969)
  Pallas kernels: 40.2 us -> 38.9 us
    pallas_call x1, Pallas kernels: 40.2 us -> 38.9 us  [local(): pl.pallas_call(kernel, out_shape=jax.ShapeDtypeStruct((64, 128), F32), in...]
where the time goes in v2:
time: 40.5 us; the launch traced here: 40.3 us
  Pallas kernels  38.9 us (96%)
  local copies, waits for them, and re-layouts  1.38 us (3%)
    pallas_call x1, Pallas kernels, local(): pl.pallas_call(kernel, out_shape=jax.ShapeDtypeStruct((64, 128), F32), in...  38.9 us
    unnamed x1, local copies, waits for them, and re-layouts  1.38 us

profile of v2, /device:TPU:1, one launch (start us, length us, event | category | flops | bytes accessed | tf_op | source)
XLA Modules:
  0.0 40.3 jit_solution(13727760090790034739)
XLA Ops:
  0.0 38.9 %shard_map.154 = f32[64,128]{1,0:T(8,128)} custom-call(bf16[64,128]{1,0:T(8,128)(2,1)} %charges_h.1, bf16[128,512]{1,0:T(8,128)(2,1)} %p2m_h.1, bf16[8,512,128]{2,1,0:T(8,128)(2,1)} %m2m_h.1, bf16[8,512,128]{2,1,0:T(8,128)(2,1)} %lops_h.1, bf16[4,512,128]{2,1,0:T(8,128)(2,1)} %cops_h.1, bf16[8,512,128]{2,1,0:T(8,128)(2,1)} %l2l_h.1, bf16[512,512]{1,0:T(8,128)(2,1)} %l2p_h.1, ...), custom_call_target="tpu_custom_call" | custom-call | tf_op jit(solution)/shard_map/pallas_call | solution.py:333
  38.9 1.4 %copy.18 = f32[64,128]{1,0:T(8,128)} copy(f32[64,128]{1,0:T(8,128)} %shard_map.154) | data formatting | bytes 65536

commit v3 on v2

--- a/solution.py
+++ b/solution.py
@@ -67,7 +67,6 @@
     sibling = (chip * 2 + other, lvl)
     right = (lax.rem(leaf + 1, 128), lvl)
     left = (lax.rem(leaf + 127, 128), lvl)
-    beside = (lax.rem(leaf + 127 + 2 * core, 128), lvl)
     near_far = (4, 3, 5, 2, 6, 1, 7)
     zpeers = [(lax.rem(z + k, 8) * 16 + y * 2 + core, lvl) for k in near_far]
     ypeers = [(z * 16 + lax.rem(y + k, 8) * 2 + core, lvl) for k in near_far]
@@ -76,7 +75,7 @@
     mine = pl.ds(pl.multiple_of(lvl * 128, 128), 128)
 
     barrier = pltpu.get_barrier_semaphore()
-    greeted = zpeers + ypeers + xpeers + across + [sibling, beside]
+    greeted = zpeers + ypeers + xpeers + [sibling]
     for peer in greeted:
         pl.semaphore_signal(barrier, inc=1, device_id=peer, device_id_type=MESH)
 
@@ -208,30 +207,10 @@
     for part in range(2):
         s_coarse[:, part * 512 : (part + 1) * 512] = counts(ccode, 512, part * 512)
 
-    loads["near"].wait()
-    loads["kind"].wait()
-    ncode = kind_v[...] * 128 + (near_v[...] - (leaf * 64 - 32))
-    s_near[...] = counts(flipped(ncode), 512, 0)
-
-    for copy in ch:
-        copy.wait_recv()
-    halo = [
-        remote(ext.at[pl.ds(64, 32)], ext.at[pl.ds(0, 32)], halo_s.at[0], halo_r.at[0], right),
-        remote(ext.at[pl.ds(32, 32)], ext.at[pl.ds(96, 32)], halo_s.at[1], halo_r.at[1], left),
-    ]
-
     own_c.wait()
     for copy in cw:
         copy.wait_recv()
     swap = [remote(coarsew.at[chalf], coarsew.at[chalf], sw_s.at[0], sw_r.at[0], sibling)]
-
-    for copy in halo:
-        copy.wait_recv()
-    loads["tiles"].wait()
-    close = jnp.zeros((64, 128), F32)
-    for t in range(4):
-        close = close + mm(s_near[:, t * 128 : (t + 1) * 128], mm(ext[...], tiles[t]).astype(BF16))
-    out_ref[...] = close
 
     own_l.wait()
     for copy in lw:
@@ -247,9 +226,18 @@
         rows = jnp.concatenate([gathered[t * 8 : t * 8 + 8], gathered[32 + t * 8 : 40 + t * 8]], axis=0)
         coarse = coarse + mm(rows, coarsew[t])
     coarse_own[...] = coarse.reshape(2, 8, 512)
-    co = [remote(coarse_own.at[0], coarse_slot.at[i], co_s.at[i], co_r.at[i], xpeers[i]) for i in range(3)]
-    co += [remote(coarse_own.at[1], coarse_slot.at[3 + i], co_s.at[3 + i], co_r.at[3 + i], across[i]) for i in range(3)]
-    co += [remote(coarse_own.at[1], coarse_slot.at[6], co_s.at[6], co_r.at[6], sibling)]
+    co = [None] * 7
+    for i in range(3):
+        co[i] = remote(coarse_own.at[0], coarse_slot.at[i], co_s.at[i], co_r.at[i], xpeers[i])
+        co[3 + i] = remote(coarse_own.at[1], coarse_slot.at[3 + i], co_s.at[3 + i], co_r.at[3 + i], across[i])
+    co[6] = remote(coarse_own.at[1], coarse_slot.at[6], co_s.at[6], co_r.at[6], sibling)
+
+    for copy in ch:
+        copy.wait_recv()
+    halo = [
+        remote(ext.at[pl.ds(64, 32)], ext.at[pl.ds(0, 32)], halo_s.at[0], halo_r.at[0], right),
+        remote(ext.at[pl.ds(32, 32)], ext.at[pl.ds(96, 32)], halo_s.at[1], halo_r.at[1], left),
+    ]
 
     def swapped(x):
         return jnp.concatenate([x[:, 4:], x[:, :4]], axis=1)
@@ -287,7 +275,19 @@
         remote(pot_out.at[lax.rem(lvl + k, 4)], pot_slot.at[i], po_s.at[i], po_r.at[i], xpeers[i])
         for i, k in enumerate(XOFF)
     ]
-    result = out_ref[...] + pot[:, mine]
+    loads["near"].wait()
+    loads["kind"].wait()
+    ncode = kind_v[...] * 128 + (near_v[...] - (leaf * 64 - 32))
+    s_near[...] = counts(flipped(ncode), 512, 0)
+
+    for copy in halo:
+        copy.wait_recv()
+    loads["tiles"].wait()
+    close = jnp.zeros((64, 128), F32)
+    for t in range(4):
+        close = close + mm(s_near[:, t * 128 : (t + 1) * 128], mm(ext[...], tiles[t]).astype(BF16))
+    result = close + pot[:, mine]
+
 
     for copy in ct + mp + ch + cw + lw + swap + halo + [sib] + co:
         copy.wait_send()

time: 40.5 us -> 39.9 us (0.985)
  Pallas kernels: 38.9 us -> 38.4 us
    pallas_call x1, Pallas kernels: 38.9 us -> 38.4 us  [local(): pl.pallas_call(kernel, out_shape=jax.ShapeDtypeStruct((64, 128), F32), in...]
where the time goes in v3:
time: 39.9 us; the launch traced here: 39.8 us
  Pallas kernels  38.4 us (96%)
  local copies, waits for them, and re-layouts  1.38 us (3%)
    pallas_call x1, Pallas kernels, local(): pl.pallas_call(kernel, out_shape=jax.ShapeDtypeStruct((64, 128), F32), in...  38.4 us
    unnamed x1, local copies, waits for them, and re-layouts  1.38 us

profile of v3, /device:TPU:1, one launch (start us, length us, event | category | flops | bytes accessed | tf_op | source)
XLA Modules:
  0.0 39.8 jit_solution(6830885177751318433)
XLA Ops:
  0.0 38.4 %shard_map.154 = f32[64,128]{1,0:T(8,128)} custom-call(bf16[64,128]{1,0:T(8,128)(2,1)} %charges_h.1, bf16[128,512]{1,0:T(8,128)(2,1)} %p2m_h.1, bf16[8,512,128]{2,1,0:T(8,128)(2,1)} %m2m_h.1, bf16[8,512,128]{2,1,0:T(8,128)(2,1)} %lops_h.1, bf16[4,512,128]{2,1,0:T(8,128)(2,1)} %cops_h.1, bf16[8,512,128]{2,1,0:T(8,128)(2,1)} %l2l_h.1, bf16[512,512]{1,0:T(8,128)(2,1)} %l2p_h.1, ...), custom_call_target="tpu_custom_call" | custom-call | tf_op jit(solution)/shard_map/pallas_call | solution.py:333
  38.4 1.4 %copy.18 = f32[64,128]{1,0:T(8,128)} copy(f32[64,128]{1,0:T(8,128)} %shard_map.154) | data formatting | bytes 65536

commit v4 on v3

--- a/solution.py
+++ b/solution.py
@@ -108,10 +108,6 @@
     pl.semaphore_wait(barrier, len(greeted))
 
     mp = [remote(mpart, mslot.at[i], mp_s.at[i], mp_r.at[i], xpeers[i]) for i in range(3)]
-    ch = [
-        remote(charges, ext.at[pl.ds(32, 64), mine], ch_s.at[i], ch_r.at[i], xpeers[i])
-        for i in range(3)
-    ]
     loads["csrc"].wait()
     loads["cop"].wait()
     ct = [remote(cells.at[0], cells.at[1], ct_s, ct_r, sibling)]
@@ -192,6 +188,10 @@
         return carry
 
     lax.fori_loop(0, 63, send_one, 0)
+    ch = [
+        remote(charges, ext.at[pl.ds(32, 64), mine], ch_s.at[i], ch_r.at[i], xpeers[i])
+        for i in range(3)
+    ]
     rbuf[pl.ds(chip, 1)] = msg[pl.ds(chip, 1)]
     pool[512:576, :] = quarter
     pool[576:640, :] = jnp.zeros((64, 128), BF16)

time: 39.9 us -> 39.9 us (level)
  no operation moved by 1% of the time
where the time goes in v4:
time: 39.9 us; the launch traced here: 39.7 us
  Pallas kernels  38.3 us (96%)
  local copies, waits for them, and re-layouts  1.38 us (3%)
    pallas_call x1, Pallas kernels, local(): pl.pallas_call(kernel, out_shape=jax.ShapeDtypeStruct((64, 128), F32), in...  38.3 us
    unnamed x1, local copies, waits for them, and re-layouts  1.38 us

profile of v4, /device:TPU:1, one launch (start us, length us, event | category | flops | bytes accessed | tf_op | source)
XLA Modules:
  0.0 39.7 jit_solution(12260532973414183042)
XLA Ops:
  0.0 38.3 %shard_map.154 = f32[64,128]{1,0:T(8,128)} custom-call(bf16[64,128]{1,0:T(8,128)(2,1)} %charges_h.1, bf16[128,512]{1,0:T(8,128)(2,1)} %p2m_h.1, bf16[8,512,128]{2,1,0:T(8,128)(2,1)} %m2m_h.1, bf16[8,512,128]{2,1,0:T(8,128)(2,1)} %lops_h.1, bf16[4,512,128]{2,1,0:T(8,128)(2,1)} %cops_h.1, bf16[8,512,128]{2,1,0:T(8,128)(2,1)} %l2l_h.1, bf16[512,512]{1,0:T(8,128)(2,1)} %l2p_h.1, ...), custom_call_target="tpu_custom_call" | custom-call | tf_op jit(solution)/shard_map/pallas_call | solution.py:333
  38.3 1.4 %copy.18 = f32[64,128]{1,0:T(8,128)} copy(f32[64,128]{1,0:T(8,128)} %shard_map.154) | data formatting | bytes 65536
